TPU v7x, 512 devices: a whole 4x8x8 slice. The times are simulated.
512 devices in a mesh: pair: 32 (over y_lo, z), day: 16 (over y_hi, x, core).
Axes of the slice: x: 4, y: 8 (y_hi: 2, y_lo: 4; y = y_hi * 4 + y_lo), z: 8, core: 2. Of those that a mesh axis runs over, the one named last changes fastest.
Arguments:
- spectra: bfloat16 [32, 2, 2048, 1024], P('day', None, 'pair'), may hold values from -6 to 6
- band_weights: float32 [8, 2048], replicated, may hold values from 0.05 to 1
- pair_stations: int32 [1536, 2], replicated, may hold values from 0 to 1023
- block_live: int32 [512], P(('pair', 'day')), may hold values from 1 to 3, 1152 in all
- windows: int32 [1536, 8, 2], P(('pair', 'day')), may hold values from 0 to 4096, as said below
- observed: bfloat16 [1536, 8, 4096], P(('pair', 'day')), may hold values from -6 to 6
Outputs:
- adjoint: float32 [32, 2, 2048, 1024], P('day', None, 'pair')
Inputs may be any that keep to these rules, and one draw needn't show every extreme that they name: Block b holds pairs b * 3 to b * 3 + 2, and its first block_live[b] pairs are live. windows[p, k, 0] < windows[p, k, 1].
All inputs are finite; a program needn't handle non-finite values.
Results may differ from a plain program's by a relative error of at most 0.0035.
Values sent between devices are 32-bit elements; how exact they have to be, the bound alone decides.
A program may use at most 64 MiB of HBM per device.

v0:
```python
import math
import jax
import jax.numpy as jnp
from jax import lax
from jax.sharding import PartitionSpec as P


def table_block(start, width, lags):
    half = lags // 2
    freqs = jnp.arange(half, dtype=jnp.int32)
    lag_index = start + jnp.arange(width, dtype=jnp.int32)
    phase = freqs[:, None] * lag_index[None, :] % lags
    angle = phase.astype(jnp.float32) * (2.0 * math.pi / lags)
    return jnp.concatenate([jnp.cos(angle), -jnp.sin(angle)], axis=0).astype(jnp.bfloat16)


def one_hot_rows(identity, columns):
    return (identity[:, None] == columns[None, :]).astype(jnp.bfloat16)


def gather_rows(flat_spectra, stations):
    count = stations.shape[0]
    station_count = flat_spectra.shape[1]
    width = math.gcd(count, 512)
    columns = jnp.arange(station_count, dtype=jnp.int32)
    dims = (((1,), (1,)), ((), ()))

    def gather_step(index, buffers):
        start = index * width
        identity = lax.dynamic_slice_in_dim(stations, start, width, 0)
        first_hot = one_hot_rows(identity[:, 0], columns)
        second_hot = one_hot_rows(identity[:, 1], columns)
        first_part = lax.dot_general(
            flat_spectra, first_hot, dims, preferred_element_type=jnp.float32
        ).astype(jnp.bfloat16)
        second_part = lax.dot_general(
            flat_spectra, second_hot, dims, preferred_element_type=jnp.float32
        ).astype(jnp.bfloat16)
        return (
            lax.dynamic_update_slice_in_dim(buffers[0], first_part, start, 1),
            lax.dynamic_update_slice_in_dim(buffers[1], second_part, start, 1),
        )

    empty = jnp.zeros((flat_spectra.shape[0], count), jnp.bfloat16)
    return lax.fori_loop(0, count // width, gather_step, (empty, empty))


def cross_stack(first_rows, second_rows, day_count, freq_count):
    count = first_rows.shape[1]
    first = first_rows.reshape(day_count, 2, freq_count, count).astype(jnp.float32)
    second = second_rows.reshape(day_count, 2, freq_count, count).astype(jnp.float32)
    real_part = jnp.sum(first[:, 0] * second[:, 0] + first[:, 1] * second[:, 1], axis=0)
    imag_part = jnp.sum(first[:, 0] * second[:, 1] - first[:, 1] * second[:, 0], axis=0)
    return jnp.stack([real_part, imag_part]).transpose(0, 2, 1)


def add_to_stations(accum, to_first, to_second, stations):
    count = stations.shape[0]
    station_count = accum.shape[1]
    width = math.gcd(count, 512)
    columns = jnp.arange(station_count, dtype=jnp.int32)

    def add_step(index, total):
        start = index * width
        identity = lax.dynamic_slice_in_dim(stations, start, width, 0)
        hot = jnp.concatenate(
            [one_hot_rows(identity[:, 0], columns), one_hot_rows(identity[:, 1], columns)], axis=0
        )
        terms = jnp.concatenate(
            [
                lax.dynamic_slice_in_dim(to_first, start, width, 1),
                lax.dynamic_slice_in_dim(to_second, start, width, 1),
            ],
            axis=1,
        )
        return total + jnp.dot(
            terms,
            hot.astype(jnp.float32),
            precision=lax.Precision.HIGHEST,
            preferred_element_type=jnp.float32,
        )

    return lax.fori_loop(0, count // width, add_step, accum)


def station_terms(accum, first_rows, second_rows, grads, stations, day_count):
    count = first_rows.shape[1]
    freq_count = grads.shape[2]
    first = first_rows.reshape(day_count, 2, freq_count, count).astype(jnp.float32)
    second = second_rows.reshape(day_count, 2, freq_count, count).astype(jnp.float32)
    turned = grads.transpose(0, 2, 1)
    grad_real = turned[0][None]
    grad_imag = turned[1][None]
    to_first = jnp.stack(
        [
            grad_real * second[:, 0] + grad_imag * second[:, 1],
            grad_real * second[:, 1] - grad_imag * second[:, 0],
        ],
        axis=1,
    ).reshape(-1, count)
    to_second = jnp.stack(
        [
            grad_real * first[:, 0] - grad_imag * first[:, 1],
            grad_real * first[:, 1] + grad_imag * first[:, 0],
        ],
        axis=1,
    ).reshape(-1, count)
    return add_to_stations(accum, to_first, to_second, stations)


def body(spectra, band_weights, pair_stations, block_live, windows, observed):
    n_pair = lax.axis_size("pair")
    n_day = lax.axis_size("day")
    per_block, bands, lags = observed.shape
    half = lags // 2
    day_count = spectra.shape[0]
    freq_count = spectra.shape[2]
    station_count = spectra.shape[3]
    days = day_count * n_day
    ordered = (
        pair_stations.reshape(n_pair, n_day, per_block, 2).transpose(1, 0, 2, 3).reshape(-1, 2)
    )
    flat_spectra = spectra.reshape(-1, station_count)
    first_rows, second_rows = gather_rows(flat_spectra, ordered)
    local_stack = cross_stack(first_rows, second_rows, day_count, freq_count)
    total = lax.psum(local_stack, "day")
    day_share = lax.dynamic_slice_in_dim(
        total, lax.axis_index("day") * (n_pair * per_block), n_pair * per_block, 1
    )
    pair_stack = lax.all_to_all(day_share, "pair", split_axis=1, concat_axis=2, tiled=True)
    weights_full = jnp.concatenate([band_weights, band_weights], axis=1)
    flat_stack = jnp.concatenate([pair_stack[0], pair_stack[1]], axis=1)
    weighted = (
        (flat_stack[:, None, :] * weights_full[None])
        .astype(jnp.bfloat16)
        .reshape(per_block * bands, lags)
    )
    live = jnp.arange(per_block, dtype=jnp.int32) < block_live[0]
    row_live = jnp.repeat(live, bands)
    lower_lag = windows[:, :, 0].reshape(-1)
    upper_lag = windows[:, :, 1].reshape(-1)
    observed_rows = observed.reshape(per_block * bands, lags)
    width = min(256, lags)
    forward_scale = 2.0 / math.sqrt(lags * days)
    adjoint_scale = 1.0 / math.sqrt(lags)

    def lag_step(index, accum):
        start = index * width
        block_table = table_block(start, width, lags)
        corr = forward_scale * jnp.dot(weighted, block_table, preferred_element_type=jnp.float32)
        lag_index = start + jnp.arange(width, dtype=jnp.int32)
        inside = (
            row_live[:, None]
            & (lag_index[None, :] >= lower_lag[:, None])
            & (lag_index[None, :] < upper_lag[:, None])
        )
        target = lax.dynamic_slice_in_dim(observed_rows, start, width, 1).astype(jnp.float32)
        misfit = jnp.where(inside, corr - target, 0.0).astype(jnp.bfloat16)
        return accum + lax.dot_general(
            misfit, block_table, (((1,), (1,)), ((), ())), preferred_element_type=jnp.float32
        )

    adjoint_rows = lax.fori_loop(
        0, lags // width, lag_step, jnp.zeros((per_block * bands, lags), jnp.float32)
    )
    summed = jnp.sum(adjoint_rows.reshape(per_block, bands, lags) * weights_full[None], axis=1)
    adjoint_spec = adjoint_scale * summed
    adjoint_split = adjoint_spec.reshape(per_block, 2, half).transpose(1, 0, 2)
    spread = lax.all_to_all(adjoint_split, "pair", split_axis=2, concat_axis=1, tiled=True)
    start_total = jnp.zeros((flat_spectra.shape[0], station_count), jnp.float32)
    all_pairs = lax.all_gather(spread, "day", axis=1, tiled=True)
    flat_out = station_terms(start_total, first_rows, second_rows, all_pairs, ordered, day_count)
    return flat_out.reshape(spectra.shape)


def solution(mesh):
    in_specs = (
        P("day", None, "pair", None),
        P(),
        P(),
        P(("pair", "day")),
        P(("pair", "day"), None, None),
        P(("pair", "day"), None, None),
    )
    out_specs = P("day", None, "pair", None)
    return jax.shard_map(body, mesh=mesh, in_specs=in_specs, out_specs=out_specs, check_vma=False)
```

profile of v0, /device:TPU:1, one launch (start us, length us, event | category | flops | bytes accessed | tf_op | source)
XLA Modules:
  0.0 495.4 jit_solution(16453960934737975883)
XLA Ops:
  6.5 1.1 reshape.62
  8.3 4.5 while.49
  13.2 1.1 copy-done
  14.8 0.9 maximum_bitcast_fusion
  16.7 188.6 %all-reduce.2.cloned.1.call-done = f32[2,1536,64]{1,2,0:T(8,128)} async-done(((f32[2,1536,64]{1,2,0:T(8,128)}), f32[2,1536,64]{1,2,0:T(8,128)}) %all-reduce.2.cloned.1.call-update) | async-done | bytes 786448 | tf_op jit(solution)/shard_map/psum | solution.py:126
  205.3 1.0 constant_dynamic-slice_fusion.4
  206.4 0.8 reshape.72
  207.2 7.7 %all-to-all-start = ((f32[32,1,384]{2,1,0:T(1,128)}), f32[32,1,384]{2,1,0:T(1,128)S(1)}, u32[]{:S(2)}, u32[]{:S(2)}) async-start(f32[32,1,384]{2,1,0:T(1,128)} %reshape.72), calls=%async_computation | async-start | bytes 98304 | tf_op jit(solution)/shard_map/all_to_all | solution.py:130
  214.9 9.1 %all-to-all-done = f32[32,1,384]{2,1,0:T(1,128)S(1)} async-done(((f32[32,1,384]{2,1,0:T(1,128)}), f32[32,1,384]{2,1,0:T(1,128)S(1)}, u32[]{:S(2)}, u32[]{:S(2)}) %all-to-all-start) | async-done | bytes 49184 | tf_op jit(solution)/shard_map/all_to_all | solution.py:130
  225.7 176.8 %while.51 = (s32[]{:T(128)}, f32[24,4096]{1,0:T(8,128)S(1)}, s32[3,8,1]{1,0,2:T(4,128)}, s32[3,8,1]{1,0,2:T(4,128)}, bf16[24,4096]{1,0:T(8,128)(2,1)}, /*index=5...) while((s32[]{:T(128)}, f32[24,4096]{1,0:T(8,128)S(1)}, ...), condition=%wide.wide.region_6.7_spmd.clone, body=%wide.wide.region_5.6_spmd.clone.sunk | while | flops 118413576 | bytes 7291664 | solution.py:163
  225.8 8.6 %cosine_convert_fusion.3 = (bf16[2048,256]{1,0:T(8,128)(2,1)S(1)}, bf16[2048,256]{1,0:T(8,128)(2,1)S(1)}) fusion(s32[256]{0:T(256)S(1)} %iota_add_fusion.3), kind=kLoop, calls=%fused_computation.26.clone.clone.1 | loop fusion | flops 8912896 | bytes 2098176 | tf_op jit(solution)/shard_map/convert.1
  234.6 2.2 convolution_add_fusion.3
  236.8 8.6 %cosine_convert_fusion.3 = (bf16[2048,256]{1,0:T(8,128)(2,1)S(1)}, bf16[2048,256]{1,0:T(8,128)(2,1)S(1)}) fusion(s32[256]{0:T(256)S(1)} %iota_add_fusion.3), kind=kLoop, calls=%fused_computation.26.clone.clone.1 | loop fusion | flops 8912896 | bytes 2098176 | tf_op jit(solution)/shard_map/convert.1
  245.6 2.2 convolution_add_fusion.3
  247.9 8.6 %cosine_convert_fusion.3 = (bf16[2048,256]{1,0:T(8,128)(2,1)S(1)}, bf16[2048,256]{1,0:T(8,128)(2,1)S(1)}) fusion(s32[256]{0:T(256)S(1)} %iota_add_fusion.3), kind=kLoop, calls=%fused_computation.26.clone.clone.1 | loop fusion | flops 8912896 | bytes 2098176 | tf_op jit(solution)/shard_map/convert.1
  256.7 2.2 convolution_add_fusion.3
  258.9 8.6 %cosine_convert_fusion.3 = (bf16[2048,256]{1,0:T(8,128)(2,1)S(1)}, bf16[2048,256]{1,0:T(8,128)(2,1)S(1)}) fusion(s32[256]{0:T(256)S(1)} %iota_add_fusion.3), kind=kLoop, calls=%fused_computation.26.clone.clone.1 | loop fusion | flops 8912896 | bytes 2098176 | tf_op jit(solution)/shard_map/convert.1
  267.7 2.2 convolution_add_fusion.3
  270.0 8.6 %cosine_convert_fusion.3 = (bf16[2048,256]{1,0:T(8,128)(2,1)S(1)}, bf16[2048,256]{1,0:T(8,128)(2,1)S(1)}) fusion(s32[256]{0:T(256)S(1)} %iota_add_fusion.3), kind=kLoop, calls=%fused_computation.26.clone.clone.1 | loop fusion | flops 8912896 | bytes 2098176 | tf_op jit(solution)/shard_map/convert.1
  278.8 2.2 convolution_add_fusion.3
  281.0 8.6 %cosine_convert_fusion.3 = (bf16[2048,256]{1,0:T(8,128)(2,1)S(1)}, bf16[2048,256]{1,0:T(8,128)(2,1)S(1)}) fusion(s32[256]{0:T(256)S(1)} %iota_add_fusion.3), kind=kLoop, calls=%fused_computation.26.clone.clone.1 | loop fusion | flops 8912896 | bytes 2098176 | tf_op jit(solution)/shard_map/convert.1
  289.8 2.2 convolution_add_fusion.3
  292.1 8.6 %cosine_convert_fusion.3 = (bf16[2048,256]{1,0:T(8,128)(2,1)S(1)}, bf16[2048,256]{1,0:T(8,128)(2,1)S(1)}) fusion(s32[256]{0:T(256)S(1)} %iota_add_fusion.3), kind=kLoop, calls=%fused_computation.26.clone.clone.1 | loop fusion | flops 8912896 | bytes 2098176 | tf_op jit(solution)/shard_map/convert.1
  300.9 2.2 convolution_add_fusion.3
  303.1 8.6 %cosine_convert_fusion.3 = (bf16[2048,256]{1,0:T(8,128)(2,1)S(1)}, bf16[2048,256]{1,0:T(8,128)(2,1)S(1)}) fusion(s32[256]{0:T(256)S(1)} %iota_add_fusion.3), kind=kLoop, calls=%fused_computation.26.clone.clone.1 | loop fusion | flops 8912896 | bytes 2098176 | tf_op jit(solution)/shard_map/convert.1
  311.9 2.2 convolution_add_fusion.3
  314.2 8.6 %cosine_convert_fusion.3 = (bf16[2048,256]{1,0:T(8,128)(2,1)S(1)}, bf16[2048,256]{1,0:T(8,128)(2,1)S(1)}) fusion(s32[256]{0:T(256)S(1)} %iota_add_fusion.3), kind=kLoop, calls=%fused_computation.26.clone.clone.1 | loop fusion | flops 8912896 | bytes 2098176 | tf_op jit(solution)/shard_map/convert.1
  323.0 2.2 convolution_add_fusion.3
  325.2 8.6 %cosine_convert_fusion.3 = (bf16[2048,256]{1,0:T(8,128)(2,1)S(1)}, bf16[2048,256]{1,0:T(8,128)(2,1)S(1)}) fusion(s32[256]{0:T(256)S(1)} %iota_add_fusion.3), kind=kLoop, calls=%fused_computation.26.clone.clone.1 | loop fusion | flops 8912896 | bytes 2098176 | tf_op jit(solution)/shard_map/convert.1
  334.0 2.2 convolution_add_fusion.3
  336.3 8.6 %cosine_convert_fusion.3 = (bf16[2048,256]{1,0:T(8,128)(2,1)S(1)}, bf16[2048,256]{1,0:T(8,128)(2,1)S(1)}) fusion(s32[256]{0:T(256)S(1)} %iota_add_fusion.3), kind=kLoop, calls=%fused_computation.26.clone.clone.1 | loop fusion | flops 8912896 | bytes 2098176 | tf_op jit(solution)/shard_map/convert.1
  345.1 2.2 convolution_add_fusion.3
  347.3 8.6 %cosine_convert_fusion.3 = (bf16[2048,256]{1,0:T(8,128)(2,1)S(1)}, bf16[2048,256]{1,0:T(8,128)(2,1)S(1)}) fusion(s32[256]{0:T(256)S(1)} %iota_add_fusion.3), kind=kLoop, calls=%fused_computation.26.clone.clone.1 | loop fusion | flops 8912896 | bytes 2098176 | tf_op jit(solution)/shard_map/convert.1
  356.1 2.2 convolution_add_fusion.3
  358.4 8.6 %cosine_convert_fusion.3 = (bf16[2048,256]{1,0:T(8,128)(2,1)S(1)}, bf16[2048,256]{1,0:T(8,128)(2,1)S(1)}) fusion(s32[256]{0:T(256)S(1)} %iota_add_fusion.3), kind=kLoop, calls=%fused_computation.26.clone.clone.1 | loop fusion | flops 8912896 | bytes 2098176 | tf_op jit(solution)/shard_map/convert.1
  367.2 2.2 convolution_add_fusion.3
  369.4 8.6 %cosine_convert_fusion.3 = (bf16[2048,256]{1,0:T(8,128)(2,1)S(1)}, bf16[2048,256]{1,0:T(8,128)(2,1)S(1)}) fusion(s32[256]{0:T(256)S(1)} %iota_add_fusion.3), kind=kLoop, calls=%fused_computation.26.clone.clone.1 | loop fusion | flops 8912896 | bytes 2098176 | tf_op jit(solution)/shard_map/convert.1
  378.2 2.2 convolution_add_fusion.3
  380.5 8.6 %cosine_convert_fusion.3 = (bf16[2048,256]{1,0:T(8,128)(2,1)S(1)}, bf16[2048,256]{1,0:T(8,128)(2,1)S(1)}) fusion(s32[256]{0:T(256)S(1)} %iota_add_fusion.3), kind=kLoop, calls=%fused_computation.26.clone.clone.1 | loop fusion | flops 8912896 | bytes 2098176 | tf_op jit(solution)/shard_map/convert.1
  389.3 2.2 convolution_add_fusion.3
  391.5 8.6 %cosine_convert_fusion.3 = (bf16[2048,256]{1,0:T(8,128)(2,1)S(1)}, bf16[2048,256]{1,0:T(8,128)(2,1)S(1)}) fusion(s32[256]{0:T(256)S(1)} %iota_add_fusion.3), kind=kLoop, calls=%fused_computation.26.clone.clone.1 | loop fusion | flops 8912896 | bytes 2098176 | tf_op jit(solution)/shard_map/convert.1
  400.3 2.2 convolution_add_fusion.3
  402.8 1.1 copy.65
  403.9 3.6 reshape.74
  407.5 3.9 all-to-all-start.1
  411.4 9.1 %all-to-all-done.1 = f32[32,1,384]{2,1,0:T(1,128)S(1)} async-done(((f32[32,1,384]{2,1,0:T(1,128)}), f32[32,1,384]{2,1,0:T(1,128)S(1)}, u32[]{:S(2)}, u32[]{:S(2)}) %all-to-all-start.1) | async-done | bytes 49184 | tf_op jit(solution)/shard_map/all_to_all | solution.py:169
  420.5 0.7 reduce.3
  421.2 3.1 reshape.75
  424.3 1.0 copy.70
  425.5 39.5 %all_gather.3 = f32[2,1536,64]{2,0,1:T(2,128)S(1)} all-gather(f32[2,96,64]{2,0,1:T(2,128)S(1)} %bitcast.109), channel_id=1, replica_groups=mesh['pair'=32,'day'=16] {'day'}, dimensions={1}, use_global_device_ids=true | all-gather | bytes 835584 | tf_op jit(solution)/shard_map/all_gather | solution.py:171
  464.9 2.2 fusion.66
  467.1 1.4 copy.68
  468.5 2.1 copy.69
  470.6 1.5 multiply_subtract_fusion
  472.1 1.2 pad_maximum_fusion.16
  473.3 1.3 pad_maximum_fusion.15
  475.0 12.5 %while.50 = (s32[]{:T(128)}, f32[256,1024]{1,0:T(8,128)S(1)}, f32[256,1536]{1,0:T(8,128)}, f32[256,1536]{1,0:T(8,128)}, s32[1536,2]{0,1:T(2,128)S(1)}, /*index=5...) while((s32[]{:T(128)}, f32[256,1024]{1,0:T(8,128)S(1)}, f32[256,1536]{1,0:T(8,128)}, ...), condition=%wide.region_9.10_spmd.clone.clone, body=%wide.region_8.9_spmd.clone.clone.sunk | while | flops 3224109056 | bytes 7352501 | solution.py:83
  475.8 1.3 constant_dynamic-slice_fusion.8
  477.1 2.1 fusion.88
  480.0 1.3 constant_dynamic-slice_fusion.8
  481.2 2.1 fusion.88
  484.1 1.3 constant_dynamic-slice_fusion.8
  485.4 2.1 fusion.88
  487.6 1.0 copy-done.10
  (124 shorter events, 13.6 us)
Async XLA Ops:
  6.5 1.8 copy-start.8
  6.5 198.8 %all-reduce.2.cloned.1.call-start = ((), (), s32[]{:S(2)}) async-start(), calls=%async_computation.2 | async-start | bytes 1572864 | tf_op jit(solution)/shard_map/psum | solution.py:126
  13.2 1.1 copy-start
  13.2 1.6 copy-start.2
  14.8 1.0 copy-start.7
  14.8 1.8 copy-start.4
  15.8 209.9 %copy-start.5 = (s32[3,8,1]{1,0,2:T(4,128)}, s32[3,8,1]{1,0,2:T(4,128)S(1)}, u32[]{:S(2)}) copy-start(s32[3,8,1]{1,0,2:T(4,128)S(1)} %copy.75) | copy-start | bytes 292
  15.9 209.8 %copy-start.6 = (s32[3,8,1]{1,0,2:T(4,128)}, s32[3,8,1]{1,0,2:T(4,128)S(1)}, u32[]{:S(2)}) copy-start(s32[3,8,1]{1,0,2:T(4,128)S(1)} %copy.76) | copy-start | bytes 292
  207.2 16.8 %all-to-all-start = ((f32[32,1,384]{2,1,0:T(1,128)}), f32[32,1,384]{2,1,0:T(1,128)S(1)}, u32[]{:S(2)}, u32[]{:S(2)}) async-start(f32[32,1,384]{2,1,0:T(1,128)} %reshape.72), calls=%async_computation | async-start | bytes 98304 | tf_op jit(solution)/shard_map/all_to_all | solution.py:130
  407.5 13.0 %all-to-all-start.1 = ((f32[32,1,384]{2,1,0:T(1,128)}), f32[32,1,384]{2,1,0:T(1,128)S(1)}, u32[]{:S(2)}, u32[]{:S(2)}) async-start(f32[32,1,384]{2,1,0:T(1,128)} %reshape.74), calls=%async_computation.1 | async-start | bytes 98304 | tf_op jit(solution)/shard_map/all_to_all | solution.py:169
  464.9 5.7 %copy-start.1 = (f32[2,2,64,1536]{3,2,1,0:T(8,128)S(1)}, f32[2,2,64,1536]{3,2,1,0:T(8,128)}, u32[]{:S(2)}) copy-start(f32[2,2,64,1536]{3,2,1,0:T(8,128)} %copy-done) | copy-start | bytes 4718596
  464.9 5.7 %copy-start.3 = (f32[2,2,64,1536]{3,2,1,0:T(8,128)S(1)}, f32[2,2,64,1536]{3,2,1,0:T(8,128)}, u32[]{:S(2)}) copy-start(f32[2,2,64,1536]{3,2,1,0:T(8,128)} %copy-done.2) | copy-start | bytes 4718596
  473.3 1.7 copy-start.9
  487.6 1.0 copy-start.10
Sparse Core Ops, SparseCore 0:
  15.9 189.3 all-reduce.1
where the time goes:
time: 497 us; the launch traced here: 495 us
  waiting for transfers between devices  207 us (42%)
  other arithmetic  148 us (30%)
  matrix products  45 us (9%)
  blocking collectives  39.5 us (8%)
  local copies, waits for them, and re-layouts  29.9 us (6%)
  between operations  14.4 us (3%)
  starting transfers between devices  11.5 us (2%)
    psum x1, waiting for transfers between devices, body(): total = lax.psum(local_stack, 'day')  189 us
    another operation x16, other arithmetic  138 us
    all_gather x1, blocking collectives, body(): all_pairs = lax.all_gather(spread, 'day', axis=1, tiled=True)  39.5 us
    dot_general x16, matrix products, lag_step(): lax.dot_general(misfit, block_table, (((1,), (1,)), ((), ())), preferred_...  35.5 us
    unnamed x29, local copies, waits for them, and re-layouts  10.3 us
  transfers between devices with their start and end apart: 3, of which 3 were waited for; matrix products, arithmetic and copies ran while one was open for 0% of the time, Pallas kernels for 0%

commit v1 on v0

--- a/solution.py
+++ b/solution.py
@@ -168,7 +168,8 @@
     adjoint_split = adjoint_spec.reshape(per_block, 2, half).transpose(1, 0, 2)
     spread = lax.all_to_all(adjoint_split, "pair", split_axis=2, concat_axis=1, tiled=True)
     start_total = jnp.zeros((flat_spectra.shape[0], station_count), jnp.float32)
-    all_pairs = lax.all_gather(spread, "day", axis=1, tiled=True)
+    stack = jnp.stack([spread] * lax.axis_size("day"))
+    all_pairs = jnp.concatenate(lax.all_to_all(stack, "day", 0, 0), axis=1)
     flat_out = station_terms(start_total, first_rows, second_rows, all_pairs, ordered, day_count)
     return flat_out.reshape(spectra.shape)
 

time: 497 us -> 495 us (level)
  blocking collectives: 39.5 us -> 12.1 us
  waiting for transfers between devices: 207 us -> 224 us
  starting transfers between devices: 11.5 us -> 17.3 us
    all_gather x1 -> x0, blocking collectives: 39.5 us -> none  [body(): all_pairs = lax.all_gather(spread, 'day', axis=1, tiled=True)]
    all_to_all x1, waiting for transfers between devices: 9.09 us -> 25.9 us  [body(): all_pairs = jnp.concatenate(lax.all_to_all(stack, 'day', 0, 0), axis=1)]
    all_to_all x0 -> x1, blocking collectives: none -> 12.1 us  [body(): lax.all_to_all(adjoint_split, 'pair', split_axis=2, concat_axis=1, tiled=...]
    all_to_all x1, starting transfers between devices: 3.85 us -> 9.63 us  [body(): all_pairs = jnp.concatenate(lax.all_to_all(stack, 'day', 0, 0), axis=1)]
where the time goes in v1:
time: 495 us; the launch traced here: 490 us
  waiting for transfers between devices  224 us (45%)
  other arithmetic  147 us (30%)
  matrix products  45 us (9%)
  local copies, waits for them, and re-layouts  30.2 us (6%)
  starting transfers between devices  17.3 us (3%)
  between operations  14.4 us (3%)
  blocking collectives  12.1 us (2%)
    psum x1, waiting for transfers between devices, body(): total = lax.psum(local_stack, 'day')  189 us
    another operation x16, other arithmetic  138 us
    dot_general x16, matrix products, lag_step(): lax.dot_general(misfit, block_table, (((1,), (1,)), ((), ())), preferred_...  35.5 us
    all_to_all x1, waiting for transfers between devices, body(): all_pairs = jnp.concatenate(lax.all_to_all(stack, 'day', 0, 0), axis=1)  25.9 us
    all_to_all x1, blocking collectives, body(): lax.all_to_all(adjoint_split, 'pair', split_axis=2, concat_axis=1, tiled=...  12.1 us
  transfers between devices with their start and end apart: 3, of which 3 were waited for; matrix products, arithmetic and copies ran while one was open for 0% of the time, Pallas kernels for 0%

profile of v1, /device:TPU:1, one launch (start us, length us, event | category | flops | bytes accessed | tf_op | source)
XLA Modules:
  0.0 490.0 jit_solution(11824388512755145945)
XLA Ops:
  6.5 1.1 reshape.71
  8.3 4.5 while.49
  13.2 1.1 copy-done
  14.8 0.9 maximum_bitcast_fusion
  16.7 188.6 %all-reduce.2.cloned.1.call-done = f32[2,1536,64]{1,2,0:T(8,128)} async-done(((f32[2,1536,64]{1,2,0:T(8,128)}), f32[2,1536,64]{1,2,0:T(8,128)}) %all-reduce.2.cloned.1.call-update) | async-done | bytes 786448 | tf_op jit(solution)/shard_map/psum | solution.py:126
  205.3 1.0 constant_dynamic-slice_fusion.4
  207.2 7.7 %all-to-all-start = ((f32[32,1,384]{2,1,0:T(1,128)}), f32[32,1,384]{2,1,0:T(1,128)S(1)}, u32[]{:S(2)}, u32[]{:S(2)}) async-start(f32[32,1,384]{2,1,0:T(1,128)} %reshape.83), calls=%async_computation | async-start | bytes 98304 | tf_op jit(solution)/shard_map/all_to_all | solution.py:130
  214.9 9.1 %all-to-all-done = f32[32,1,384]{2,1,0:T(1,128)S(1)} async-done(((f32[32,1,384]{2,1,0:T(1,128)}), f32[32,1,384]{2,1,0:T(1,128)S(1)}, u32[]{:S(2)}, u32[]{:S(2)}) %all-to-all-start) | async-done | bytes 49184 | tf_op jit(solution)/shard_map/all_to_all | solution.py:130
  224.5 0.8 reduce.2
  225.7 176.8 %while.51 = (s32[]{:T(128)}, f32[24,4096]{1,0:T(8,128)S(1)}, s32[3,8,1]{1,0,2:T(4,128)}, s32[3,8,1]{1,0,2:T(4,128)}, bf16[24,4096]{1,0:T(8,128)(2,1)}, /*index=5...) while((s32[]{:T(128)}, f32[24,4096]{1,0:T(8,128)S(1)}, ...), condition=%wide.wide.region_6.7_spmd.clone, body=%wide.wide.region_5.6_spmd.clone.sunk | while | flops 118413576 | bytes 7291664 | solution.py:163
  225.7 8.6 %cosine_convert_fusion.3 = (bf16[2048,256]{1,0:T(8,128)(2,1)S(1)}, bf16[2048,256]{1,0:T(8,128)(2,1)S(1)}) fusion(s32[256]{0:T(256)S(1)} %iota_add_fusion.3), kind=kLoop, calls=%fused_computation.26.clone.clone.1 | loop fusion | flops 8912896 | bytes 2098176 | tf_op jit(solution)/shard_map/convert.1
  234.5 2.2 convolution_add_fusion.3
  236.8 8.6 %cosine_convert_fusion.3 = (bf16[2048,256]{1,0:T(8,128)(2,1)S(1)}, bf16[2048,256]{1,0:T(8,128)(2,1)S(1)}) fusion(s32[256]{0:T(256)S(1)} %iota_add_fusion.3), kind=kLoop, calls=%fused_computation.26.clone.clone.1 | loop fusion | flops 8912896 | bytes 2098176 | tf_op jit(solution)/shard_map/convert.1
  245.6 2.2 convolution_add_fusion.3
  247.8 8.6 %cosine_convert_fusion.3 = (bf16[2048,256]{1,0:T(8,128)(2,1)S(1)}, bf16[2048,256]{1,0:T(8,128)(2,1)S(1)}) fusion(s32[256]{0:T(256)S(1)} %iota_add_fusion.3), kind=kLoop, calls=%fused_computation.26.clone.clone.1 | loop fusion | flops 8912896 | bytes 2098176 | tf_op jit(solution)/shard_map/convert.1
  256.6 2.2 convolution_add_fusion.3
  258.9 8.6 %cosine_convert_fusion.3 = (bf16[2048,256]{1,0:T(8,128)(2,1)S(1)}, bf16[2048,256]{1,0:T(8,128)(2,1)S(1)}) fusion(s32[256]{0:T(256)S(1)} %iota_add_fusion.3), kind=kLoop, calls=%fused_computation.26.clone.clone.1 | loop fusion | flops 8912896 | bytes 2098176 | tf_op jit(solution)/shard_map/convert.1
  267.7 2.2 convolution_add_fusion.3
  269.9 8.6 %cosine_convert_fusion.3 = (bf16[2048,256]{1,0:T(8,128)(2,1)S(1)}, bf16[2048,256]{1,0:T(8,128)(2,1)S(1)}) fusion(s32[256]{0:T(256)S(1)} %iota_add_fusion.3), kind=kLoop, calls=%fused_computation.26.clone.clone.1 | loop fusion | flops 8912896 | bytes 2098176 | tf_op jit(solution)/shard_map/convert.1
  278.7 2.2 convolution_add_fusion.3
  281.0 8.6 %cosine_convert_fusion.3 = (bf16[2048,256]{1,0:T(8,128)(2,1)S(1)}, bf16[2048,256]{1,0:T(8,128)(2,1)S(1)}) fusion(s32[256]{0:T(256)S(1)} %iota_add_fusion.3), kind=kLoop, calls=%fused_computation.26.clone.clone.1 | loop fusion | flops 8912896 | bytes 2098176 | tf_op jit(solution)/shard_map/convert.1
  289.8 2.2 convolution_add_fusion.3
  292.0 8.6 %cosine_convert_fusion.3 = (bf16[2048,256]{1,0:T(8,128)(2,1)S(1)}, bf16[2048,256]{1,0:T(8,128)(2,1)S(1)}) fusion(s32[256]{0:T(256)S(1)} %iota_add_fusion.3), kind=kLoop, calls=%fused_computation.26.clone.clone.1 | loop fusion | flops 8912896 | bytes 2098176 | tf_op jit(solution)/shard_map/convert.1
  300.8 2.2 convolution_add_fusion.3
  303.1 8.6 %cosine_convert_fusion.3 = (bf16[2048,256]{1,0:T(8,128)(2,1)S(1)}, bf16[2048,256]{1,0:T(8,128)(2,1)S(1)}) fusion(s32[256]{0:T(256)S(1)} %iota_add_fusion.3), kind=kLoop, calls=%fused_computation.26.clone.clone.1 | loop fusion | flops 8912896 | bytes 2098176 | tf_op jit(solution)/shard_map/convert.1
  311.9 2.2 convolution_add_fusion.3
  314.1 8.6 %cosine_convert_fusion.3 = (bf16[2048,256]{1,0:T(8,128)(2,1)S(1)}, bf16[2048,256]{1,0:T(8,128)(2,1)S(1)}) fusion(s32[256]{0:T(256)S(1)} %iota_add_fusion.3), kind=kLoop, calls=%fused_computation.26.clone.clone.1 | loop fusion | flops 8912896 | bytes 2098176 | tf_op jit(solution)/shard_map/convert.1
  322.9 2.2 convolution_add_fusion.3
  325.2 8.6 %cosine_convert_fusion.3 = (bf16[2048,256]{1,0:T(8,128)(2,1)S(1)}, bf16[2048,256]{1,0:T(8,128)(2,1)S(1)}) fusion(s32[256]{0:T(256)S(1)} %iota_add_fusion.3), kind=kLoop, calls=%fused_computation.26.clone.clone.1 | loop fusion | flops 8912896 | bytes 2098176 | tf_op jit(solution)/shard_map/convert.1
  334.0 2.2 convolution_add_fusion.3
  336.2 8.6 %cosine_convert_fusion.3 = (bf16[2048,256]{1,0:T(8,128)(2,1)S(1)}, bf16[2048,256]{1,0:T(8,128)(2,1)S(1)}) fusion(s32[256]{0:T(256)S(1)} %iota_add_fusion.3), kind=kLoop, calls=%fused_computation.26.clone.clone.1 | loop fusion | flops 8912896 | bytes 2098176 | tf_op jit(solution)/shard_map/convert.1
  345.0 2.2 convolution_add_fusion.3
  347.3 8.6 %cosine_convert_fusion.3 = (bf16[2048,256]{1,0:T(8,128)(2,1)S(1)}, bf16[2048,256]{1,0:T(8,128)(2,1)S(1)}) fusion(s32[256]{0:T(256)S(1)} %iota_add_fusion.3), kind=kLoop, calls=%fused_computation.26.clone.clone.1 | loop fusion | flops 8912896 | bytes 2098176 | tf_op jit(solution)/shard_map/convert.1
  356.1 2.2 convolution_add_fusion.3
  358.3 8.6 %cosine_convert_fusion.3 = (bf16[2048,256]{1,0:T(8,128)(2,1)S(1)}, bf16[2048,256]{1,0:T(8,128)(2,1)S(1)}) fusion(s32[256]{0:T(256)S(1)} %iota_add_fusion.3), kind=kLoop, calls=%fused_computation.26.clone.clone.1 | loop fusion | flops 8912896 | bytes 2098176 | tf_op jit(solution)/shard_map/convert.1
  367.1 2.2 convolution_add_fusion.3
  369.4 8.6 %cosine_convert_fusion.3 = (bf16[2048,256]{1,0:T(8,128)(2,1)S(1)}, bf16[2048,256]{1,0:T(8,128)(2,1)S(1)}) fusion(s32[256]{0:T(256)S(1)} %iota_add_fusion.3), kind=kLoop, calls=%fused_computation.26.clone.clone.1 | loop fusion | flops 8912896 | bytes 2098176 | tf_op jit(solution)/shard_map/convert.1
  378.2 2.2 convolution_add_fusion.3
  380.4 8.6 %cosine_convert_fusion.3 = (bf16[2048,256]{1,0:T(8,128)(2,1)S(1)}, bf16[2048,256]{1,0:T(8,128)(2,1)S(1)}) fusion(s32[256]{0:T(256)S(1)} %iota_add_fusion.3), kind=kLoop, calls=%fused_computation.26.clone.clone.1 | loop fusion | flops 8912896 | bytes 2098176 | tf_op jit(solution)/shard_map/convert.1
  389.2 2.2 convolution_add_fusion.3
  391.5 8.6 %cosine_convert_fusion.3 = (bf16[2048,256]{1,0:T(8,128)(2,1)S(1)}, bf16[2048,256]{1,0:T(8,128)(2,1)S(1)}) fusion(s32[256]{0:T(256)S(1)} %iota_add_fusion.3), kind=kLoop, calls=%fused_computation.26.clone.clone.1 | loop fusion | flops 8912896 | bytes 2098176 | tf_op jit(solution)/shard_map/convert.1
  400.3 2.2 convolution_add_fusion.3
  402.8 1.1 copy.62
  403.9 3.0 reshape.85
  406.9 12.1 %all_to_all.35 = f32[32,1,384]{2,1,0:T(1,128)S(1)} all-to-all(f32[32,1,384]{2,1,0:T(1,128)S(1)} %reshape.85), channel_id=1, replica_groups=mesh['pair'=32,'day'=16] {'pair'}, dimensions={0} | all-to-all | bytes 98304 | tf_op jit(solution)/shard_map/all_to_all | solution.py:169
  418.9 0.8 reduce.3
  419.7 3.1 reshape.86
  422.8 1.0 copy.67
  424.0 1.1 stack.18
  425.2 9.6 %all-to-all-start.2 = ((f32[16,2,96,64]{2,3,1,0:T(8,128)}), f32[16,2,96,64]{2,3,1,0:T(8,128)S(1)}, u32[]{:S(2)}, u32[]{:S(2)}) async-start(f32[16,2,96,64]{2,3,1,0:T(8,128)} %stack.18), calls=%async_computation.2 | async-start | bytes 2097152 | tf_op jit(solution)/shard_map/all_to_all | solution.py:172
  434.8 25.9 %all-to-all-done.2 = f32[16,2,96,64]{2,3,1,0:T(8,128)S(1)} async-done(((f32[16,2,96,64]{2,3,1,0:T(8,128)}), f32[16,2,96,64]{2,3,1,0:T(8,128)S(1)}, u32[]{:S(2)}, u32[]{:S(2)}) %all-to-all-start.2) | async-done | bytes 786464 | tf_op jit(solution)/shard_map/all_to_all | solution.py:172
  460.7 1.6 copy.66
  462.3 2.7 reshape.77
  465.0 1.2 slice_bitcast_fusion.1
  466.7 1.2 pad_maximum_fusion.16
  467.9 1.3 pad_maximum_fusion.15
  469.6 12.5 %while.50 = (s32[]{:T(128)}, f32[256,1024]{1,0:T(8,128)S(1)}, f32[256,1536]{1,0:T(8,128)}, f32[256,1536]{1,0:T(8,128)}, s32[1536,2]{0,1:T(2,128)S(1)}, /*index=5...) while((s32[]{:T(128)}, f32[256,1024]{1,0:T(8,128)S(1)}, f32[256,1536]{1,0:T(8,128)}, ...), condition=%wide.region_9.10_spmd.clone.clone, body=%wide.region_8.9_spmd.clone.clone.sunk | while | flops 3224109056 | bytes 7352501 | solution.py:83
  470.4 1.3 constant_dynamic-slice_fusion.8
  471.7 2.1 fusion.87
  474.6 1.3 constant_dynamic-slice_fusion.8
  475.8 2.1 fusion.87
  478.7 1.3 constant_dynamic-slice_fusion.8
  480.0 2.1 fusion.87
  482.2 1.0 copy-done.10
  (126 shorter events, 14.1 us)
Async XLA Ops:
  6.5 1.8 copy-start.8
  6.5 198.8 %all-reduce.2.cloned.1.call-start = ((), (), s32[]{:S(2)}) async-start(), calls=%async_computation.3 | async-start | bytes 1572864 | tf_op jit(solution)/shard_map/psum | solution.py:126
  13.2 1.1 copy-start
  13.2 1.6 copy-start.2
  14.8 1.0 copy-start.7
  14.8 1.8 copy-start.4
  15.8 209.9 %copy-start.5 = (s32[3,8,1]{1,0,2:T(4,128)}, s32[3,8,1]{1,0,2:T(4,128)S(1)}, u32[]{:S(2)}) copy-start(s32[3,8,1]{1,0,2:T(4,128)S(1)} %copy.72) | copy-start | bytes 292
  15.9 209.8 %copy-start.6 = (s32[3,8,1]{1,0,2:T(4,128)}, s32[3,8,1]{1,0,2:T(4,128)S(1)}, u32[]{:S(2)}) copy-start(s32[3,8,1]{1,0,2:T(4,128)S(1)} %copy.73) | copy-start | bytes 292
  207.2 16.8 %all-to-all-start = ((f32[32,1,384]{2,1,0:T(1,128)}), f32[32,1,384]{2,1,0:T(1,128)S(1)}, u32[]{:S(2)}, u32[]{:S(2)}) async-start(f32[32,1,384]{2,1,0:T(1,128)} %reshape.83), calls=%async_computation | async-start | bytes 98304 | tf_op jit(solution)/shard_map/all_to_all | solution.py:130
  425.2 35.5 %all-to-all-start.2 = ((f32[16,2,96,64]{2,3,1,0:T(8,128)}), f32[16,2,96,64]{2,3,1,0:T(8,128)S(1)}, u32[]{:S(2)}, u32[]{:S(2)}) async-start(f32[16,2,96,64]{2,3,1,0:T(8,128)} %stack.18), calls=%async_computation.2 | async-start | bytes 2097152 | tf_op jit(solution)/shard_map/all_to_all | solution.py:172
  462.3 3.9 copy-start.1
  462.3 3.9 copy-start.3
  467.9 1.7 copy-start.9
  482.2 1.0 copy-start.10
Sparse Core Ops, SparseCore 0:
  15.9 189.3 all-reduce.1
